TPU v7x, 32 devices: a whole 2x2x4 slice. The times are simulated.
32 devices in a mesh: groups: 2 (over y), dp: 4 (over z), tensor: 4 (over x, core).
Axes of the slice: x: 2, y: 2, z: 4, core: 2. Of those that a mesh axis runs over, the one named last changes fastest.
Arguments:
- normed: bfloat16 [2048, 8192], P(('groups', 'dp'), 'tensor'), parts along dimension 0, may hold values from -6 to 6
- grad_key: bfloat16 [2048, 1024], P(('groups', 'dp'), 'tensor'), parts along dimension 0, may hold values from -6 to 6
- grad_value: bfloat16 [2048, 1024], P(('groups', 'dp'), 'tensor'), parts along dimension 0, may hold values from -6 to 6
- weight_key: bfloat16 [8192, 1024], P('dp', 'tensor'), may hold values from -0.1875 to 0.1875
- weight_value: bfloat16 [8192, 1024], P('dp', 'tensor'), may hold values from -0.1875 to 0.1875
- proj_in: bfloat16 [8192, 128], P('tensor'), may hold values from -0.0625 to 0.0625
- proj_out: bfloat16 [2, 1024, 64], P(None, 'tensor'), may hold values from -0.1875 to 0.1875
- lengths: int32 [8], P(('groups', 'dp')), parts along dimension 0, may hold values from 64 to 256
- queries: bfloat16 [512, 2, 4096], P('dp', None, 'tensor'), may hold values from -6 to 6
Outputs:
- grad_input: bfloat16 [2048, 8192], P(('groups', 'dp'), 'tensor'), parts along dimension 0
- scores: float32 [512, 8], P('dp', 'groups'), parts along dimension 1
There are 2 independent parts, one for each index of `groups`. A program takes and returns all parts, laid end to end along the dimension named above; an argument that names none is the same for every part. Nothing has to cross between parts.
All inputs are finite; a program needn't handle non-finite values.
Results may differ from a plain program's by a relative error of at most 0.018.
Values may be sent and summed in bfloat16 or wider, within the bound.
A program may use at most 64 MiB of HBM per device.

v0:
```python
import jax
import jax.numpy as jnp
from jax import lax
from jax.sharding import PartitionSpec as P


def body(
    normed, grad_key, grad_value, weight_key, weight_value, proj_in, proj_out, lengths, queries
):
    grads = jnp.concatenate([grad_key, grad_value], axis=1)
    weights = jnp.concatenate([weight_key, weight_value], axis=1)
    partial_grad = lax.dot_general(
        grads,
        lax.all_gather(weights, "dp", axis=0, tiled=True),
        (((1,), (1,)), ((), ())),
        preferred_element_type=jnp.float32,
    )
    grad_input = lax.psum_scatter(
        partial_grad.astype(jnp.bfloat16), "tensor", scatter_dimension=1, tiled=True
    )
    tokens = normed.shape[0]
    rank = proj_out.shape[2]
    shards = lax.axis_size("tensor")
    own_rows = rank // shards
    in_part = jnp.dot(normed, proj_in, preferred_element_type=jnp.float32)
    out_part = jnp.stack(
        [
            jnp.dot(grad_key, proj_out[0], preferred_element_type=jnp.float32),
            jnp.dot(grad_value, proj_out[1], preferred_element_type=jnp.float32),
        ],
        axis=1,
    )
    in_whole, out_whole = (
        lax.psum(in_part.astype(jnp.bfloat16), "tensor").astype(jnp.float32),
        lax.psum(out_part.astype(jnp.bfloat16), "tensor").astype(jnp.float32),
    )
    out_own = lax.dynamic_slice_in_dim(out_whole, lax.axis_index("tensor") * own_rows, own_rows, 2)
    in_sketch = in_whole.astype(jnp.bfloat16)
    out_sketch = out_own.astype(jnp.bfloat16)
    seq_count = lengths.shape[0]
    seq_len = tokens // seq_count
    positions = lax.broadcasted_iota(jnp.int32, (seq_count, seq_len), 1)
    live = (positions < lengths[:, None]).astype(jnp.bfloat16)
    in_seq = in_sketch.reshape(seq_count, seq_len, 2, rank)
    out_seq = out_sketch.reshape(seq_count, seq_len, 2, own_rows) * live[:, :, None, None]
    sums = jnp.einsum("stla,stlb->slab", out_seq, in_seq, preferred_element_type=jnp.float32)
    scale = 1.0 / jnp.sqrt(lengths.astype(jnp.float32))
    seq_sketch = (
        (sums * scale[:, None, None, None])
        .astype(jnp.bfloat16)
        .reshape(seq_count, 2, own_rows * rank)
    )
    partial_scores = jnp.einsum(
        "qlf,slf->qs",
        queries,
        lax.all_gather(seq_sketch, "dp", axis=0, tiled=True),
        preferred_element_type=jnp.float32,
    )
    scores = lax.psum(partial_scores, "tensor") / rank
    return (grad_input, scores)


def solution(mesh):
    in_specs = (
        P(("groups", "dp"), "tensor"),
        P(("groups", "dp"), "tensor"),
        P(("groups", "dp"), "tensor"),
        P("dp", "tensor"),
        P("dp", "tensor"),
        P("tensor", None),
        P(None, "tensor", None),
        P(("groups", "dp")),
        P("dp", None, "tensor"),
    )
    out_specs = (P(("groups", "dp"), "tensor"), P("dp", "groups"))
    return jax.shard_map(body, mesh=mesh, in_specs=in_specs, out_specs=out_specs, check_vma=False)
```

profile of v0, /device:TPU:0, one launch (start us, length us, event | category | flops | bytes accessed | tf_op | source)
XLA Modules:
  0.0 221.9 jit_solution(9539174968826876651)
XLA Ops:
  8.0 0.0 copy-start
  8.0 0.0 copy-start.1
  8.0 0.0 copy-start.5
  8.0 0.0 copy-start.2
  8.0 0.0 copy-start.3
  8.1 0.0 all-gather.2.cloned.1.call-start
  8.1 3.2 %pad_maximum_fusion = bf16[2048,512]{1,0:T(8,128)(2,1)} fusion(bf16[2048,256]{1,0:T(8,128)(2,1)} %param.13, bf16[2048,256]{1,0:T(8,128)(2,1)} %param.12), kind=kLoop, calls=%fused_computation.1 | loop fusion | flops 4194304 | bytes 4194304 | tf_op jit(solution)/shard_map/concatenate | solution.py:11
  11.3 0.0 all-gather.2.cloned.1.call-update
  11.3 0.0 all-reduce.3.cloned.1.call-start
  11.4 0.0 copy-done.1
  11.4 0.0 copy-done.5
  11.4 0.2 fusion.1
  11.5 0.0 copy-done.2
  11.5 0.2 fusion
  11.7 0.7 pad_maximum_fusion.1
  12.4 0.0 copy-done
  12.4 0.0 copy-done.3
  12.4 1.1 convolution_convert_fusion.1
  13.5 0.0 all-reduce.3.cloned.1.call-update
  13.5 0.0 reduce-scatter.2.cloned.1.call-start
  13.6 150.2 %all-gather.2.cloned.1.call-done = bf16[8192,512]{1,0:T(8,128)(2,1)} async-done(((bf16[2048,512]{1,0:T(8,128)(2,1)}), bf16[8192,512]{1,0:T(8,128)(2,1)}) %all-gather.2.cloned.1.call-update) | async-done | bytes 8388624 | tf_op jit(solution)/shard_map/all_gather | solution.py:14
  163.8 7.7 %convolution_convert_fusion = bf16[256,8192]{1,0:T(8,128)(2,1)} fusion(bf16[8192,512]{1,0:T(8,128)(2,1)} %all-gather.2.cloned.1.call-done, bf16[256,256]{1,0:T(8,128)(2,1)S(1)} %copy-done.1, bf16[256,256]{1,0:T(8,128)(2,1)S(1)} %copy-done.2), kind=kOutput, calls=%fused_computation | convolution fusion | flops 2150105088 | bytes 12845056 | tf_op jit(solution)/shard_map/dot_general | solution.py:12
  171.5 0.0 copy-start.4
  171.5 0.0 reduce-scatter.2.cloned.1.call-update
  172.3 0.0 all-reduce.3.cloned.1.call-done
  172.3 1.0 fusion.2
  173.3 0.1 reshape.37
  173.4 13.1 %all_gather.7 = bf16[4,2,1024]{2,1,0:T(2,128)(2,1)S(1)} all-gather(bf16[1,2,1024]{2,1,0:T(2,128)(2,1)S(1)} %reshape.37), channel_id=1, replica_groups=mesh['groups'=2,'dp'=4,'tensor'=4] {'dp'}, dimensions={0}, use_global_device_ids=true | all-gather | bytes 20480 | tf_op jit(solution)/shard_map/all_gather | solution.py:56
  186.5 0.0 copy-done.4
  186.6 0.2 convolution_bitcast_fusion
  186.8 6.1 %psum.23 = f32[128,4]{0,1:T(4,128)S(1)} all-reduce(f32[128,4]{0,1:T(4,128)S(1)} %convolution_bitcast_fusion), channel_id=1, replica_groups=mesh['groups'=2,'dp'=4,'tensor'=4] {'tensor'}, use_global_device_ids=true, to_apply=%region_3.0 | all-reduce | flops 512 | bytes 4096 | tf_op jit(solution)/shard_map/psum | solution.py:59
  192.9 0.6 broadcast_multiply_fusion
  193.5 20.9 %reduce-scatter.2.cloned.1.call-done = bf16[256,2048]{1,0:T(8,128)(2,1)} async-done(((bf16[256,8192]{1,0:T(8,128)(2,1)}), bf16[256,2048]{1,0:T(8,128)(2,1)}) %reduce-scatter.2.cloned.1.call-update) | async-done | bytes 1048592 | tf_op jit(solution)/shard_map/reduce_scatter | solution.py:18
  (1 shorter events, 0.0 us)
Async XLA Ops:
  8.0 4.4 %copy-start = (bf16[256,2048]{1,0:T(8,128)(2,1)S(1)}, bf16[256,2048]{1,0:T(8,128)(2,1)}, u32[]{:S(2)}) copy-start(bf16[256,2048]{1,0:T(8,128)(2,1)} %param.9) | copy-start | bytes 3145732
  8.0 3.3 %copy-start.1 = (bf16[256,256]{1,0:T(8,128)(2,1)S(1)}, bf16[256,256]{1,0:T(8,128)(2,1)}, u32[]{:S(2)}) copy-start(bf16[256,256]{1,0:T(8,128)(2,1)} %param.11) | copy-start | bytes 393220
  8.0 3.3 %copy-start.5 = (bf16[2,256,64]{1,2,0:T(8,128)(2,1)S(1)}, bf16[2,256,64]{1,2,0:T(8,128)(2,1)}, u32[]{:S(2)}) copy-start(bf16[2,256,64]{1,2,0:T(8,128)(2,1)} %param.15) | copy-start | bytes 196612
  8.0 3.5 %copy-start.2 = (bf16[256,256]{1,0:T(8,128)(2,1)S(1)}, bf16[256,256]{1,0:T(8,128)(2,1)}, u32[]{:S(2)}) copy-start(bf16[256,256]{1,0:T(8,128)(2,1)} %param.10) | copy-start | bytes 393220
  8.0 4.4 %copy-start.3 = (bf16[2048,128]{1,0:T(8,128)(2,1)S(1)}, bf16[2048,128]{1,0:T(8,128)(2,1)}, u32[]{:S(2)}) copy-start(bf16[2048,128]{1,0:T(8,128)(2,1)} %param.14) | copy-start | bytes 1572868
  8.1 155.7 %all-gather.2.cloned.1.call-start = ((), (), s32[]{:S(2)}) async-start(), calls=%async_computation.1 | async-start | bytes 10485760 | tf_op jit(solution)/shard_map/all_gather | solution.py:14
  11.3 161.0 %all-reduce.3.cloned.1.call-start = ((), (), s32[]{:S(2)}) async-start(), calls=%async_computation.3 | async-start | bytes 262144 | tf_op jit(solution)/shard_map/psum | solution.py:34
  13.5 200.9 %reduce-scatter.2.cloned.1.call-start = ((), (), s32[]{:S(2)}) async-start(), calls=%async_computation.2 | async-start | bytes 5242880 | tf_op jit(solution)/shard_map/reduce_scatter | solution.py:18
  171.5 15.0 %copy-start.4 = (bf16[128,2,1024]{2,1,0:T(2,128)(2,1)S(1)}, bf16[128,2,1024]{2,1,0:T(2,128)(2,1)}, u32[]{:S(2)}) copy-start(bf16[128,2,1024]{2,1,0:T(2,128)(2,1)} %param.17) | copy-start | bytes 1572868
Sparse Core Ops, SparseCore 0:
  11.4 152.3 all-gather.1
Sparse Core Ops, SparseCore 1:
  14.2 34.1 all-reduce.2
  171.6 42.7 reduce-scatter.1
where the time goes:
time: 222 us
  waiting for transfers between devices  171 us (77%)
  blocking collectives  19.2 us (9%)
  between operations  16.3 us (7%)
  matrix products  10.4 us (5%)
  other arithmetic  4.45 us (2%)
    all_gather x1, waiting for transfers between devices, body(): lax.all_gather(weights, 'dp', axis=0, tiled=True)  150 us
    reduce_scatter x1, waiting for transfers between devices, body(): lax.psum_scatter(partial_grad.astype(jnp.bfloat16), 'tensor', scatter_dim...  20.9 us
    all_gather x1, blocking collectives, body(): lax.all_gather(seq_sketch, 'dp', axis=0, tiled=True)  13.1 us
    dot_general x1, matrix products, body(): lax.dot_general(grads, lax.all_gather(weights, 'dp', axis=0, tiled=True),...  7.72 us
    psum x1, blocking collectives, body(): scores = lax.psum(partial_scores, 'tensor') / rank  6.11 us
  transfers between devices with their start and end apart: 3, of which 2 were waited for; matrix products, arithmetic and copies ran while one was open for 5% of the time, Pallas kernels for 0%

commit v1 on v0

--- a/solution.py
+++ b/solution.py
@@ -2,6 +2,33 @@
 import jax.numpy as jnp
 from jax import lax
 from jax.sharding import PartitionSpec as P
+
+
+def by_tokens(grads, weights):
+    partial_grad = lax.dot_general(
+        grads,
+        lax.all_gather(weights, "dp", axis=0, tiled=True),
+        (((1,), (1,)), ((), ())),
+        preferred_element_type=jnp.float32,
+    )
+    return lax.psum_scatter(
+        partial_grad.astype(jnp.bfloat16), "tensor", scatter_dimension=1, tiled=True
+    )
+
+
+def by_features(grads, weights):
+    n = lax.axis_size("dp")
+    partial_grad = lax.dot_general(
+        lax.all_gather(grads, "dp", axis=0, tiled=True),
+        weights,
+        (((1,), (1,)), ((), ())),
+        preferred_element_type=jnp.float32,
+    )
+    mine = lax.psum_scatter(
+        partial_grad.astype(jnp.bfloat16), "tensor", scatter_dimension=0, tiled=True
+    )
+    turn = [(d * n + t, t * n + d) for d in range(n) for t in range(n)]
+    return lax.ppermute(mine, ("dp", "tensor"), turn)
 
 
 def body(
@@ -9,15 +36,10 @@
 ):
     grads = jnp.concatenate([grad_key, grad_value], axis=1)
     weights = jnp.concatenate([weight_key, weight_value], axis=1)
-    partial_grad = lax.dot_general(
-        grads,
-        lax.all_gather(weights, "dp", axis=0, tiled=True),
-        (((1,), (1,)), ((), ())),
-        preferred_element_type=jnp.float32,
-    )
-    grad_input = lax.psum_scatter(
-        partial_grad.astype(jnp.bfloat16), "tensor", scatter_dimension=1, tiled=True
-    )
+    if lax.axis_size("dp") == lax.axis_size("tensor"):
+        grad_input = by_features(grads, weights)
+    else:
+        grad_input = by_tokens(grads, weights)
     tokens = normed.shape[0]
     rank = proj_out.shape[2]
     shards = lax.axis_size("tensor")

time: 222 us -> 162 us (0.73)
  waiting for transfers between devices: 171 us -> 107 us
  blocking collectives: 19.2 us -> 24.4 us
    all_gather x1, waiting for transfers between devices: 150 us -> 31.8 us  [by_features(): lax.all_gather(grads, 'dp', axis=0, tiled=True)]
    psum x1, waiting for transfers between devices: 0.03 us -> 32.3 us  [body(): lax.psum(in_part.astype(jnp.bfloat16), 'tensor').astype(jnp.float32)]
    reduce_scatter x1, waiting for transfers between devices: 20.9 us -> 42.9 us  [by_features(): lax.psum_scatter(partial_grad.astype(jnp.bfloat16), 'tensor', scatter_dim...]
    all_gather x1, blocking collectives: 13.1 us -> 17 us  [body(): lax.all_gather(seq_sketch, 'dp', axis=0, tiled=True)]
  transfers between devices with their start and end apart: 3 -> 4, of which waited for: 2 -> 3; matrix products, arithmetic and copies ran while one was open for 5% -> 2% of each run, Pallas kernels for 0% -> 0%
where the time goes in v1:
time: 162 us
  waiting for transfers between devices  107 us (66%)
  blocking collectives  24.4 us (15%)
  between operations  14.5 us (9%)
  matrix products  8.86 us (5%)
  other arithmetic  2.99 us (2%)
  starting transfers between devices  1.99 us (1%)
  local copies, waits for them, and re-layouts  1.89 us (1%)
    reduce_scatter x1, waiting for transfers between devices, by_features(): lax.psum_scatter(partial_grad.astype(jnp.bfloat16), 'tensor', scatter_dim...  42.9 us
    psum x1, waiting for transfers between devices, body(): lax.psum(in_part.astype(jnp.bfloat16), 'tensor').astype(jnp.float32)  32.3 us
    all_gather x1, waiting for transfers between devices, by_features(): lax.all_gather(grads, 'dp', axis=0, tiled=True)  31.8 us
    all_gather x1, blocking collectives, body(): lax.all_gather(seq_sketch, 'dp', axis=0, tiled=True)  17 us
    psum x1, blocking collectives, body(): scores = lax.psum(partial_scores, 'tensor') / rank  7.46 us
    dot_general x1, matrix products, by_features(): lax.dot_general(lax.all_gather(grads, 'dp', axis=0, tiled=True), weights,...  6.18 us
  transfers between devices with their start and end apart: 4, of which 3 were waited for; matrix products, arithmetic and copies ran while one was open for 2% of the time, Pallas kernels for 0%

profile of v1, /device:TPU:0, one launch (start us, length us, event | category | flops | bytes accessed | tf_op | source)
XLA Modules:
  0.0 161.7 jit_solution(6338704432474040889)
XLA Ops:
  7.2 0.0 copy-start
  7.2 0.0 all-gather.2.cloned.1.call-start
  7.2 1.8 %pad_maximum_fusion = bf16[256,512]{1,0:T(8,128)(2,1)} fusion(bf16[256,256]{1,0:T(8,128)(2,1)} %param.11, bf16[256,256]{1,0:T(8,128)(2,1)} %param.10), kind=kLoop, calls=%fused_computation.13 | loop fusion | flops 524288 | bytes 524288 | tf_op jit(solution)/shard_map/concatenate | solution.py:37
  9.0 0.0 all-gather.2.cloned.1.call-update
  9.0 0.0 reduce-scatter.2.cloned.1.call-start
  9.1 31.8 %all-gather.2.cloned.1.call-done = bf16[1024,512]{1,0:T(8,128)(2,1)} async-done(((bf16[256,512]{1,0:T(8,128)(2,1)}), bf16[1024,512]{1,0:T(8,128)(2,1)}) %all-gather.2.cloned.1.call-update) | async-done | bytes 1048592 | tf_op jit(solution)/shard_map/all_gather | solution.py:22
  40.8 6.2 %convolution_convert_fusion = bf16[1024,2048]{1,0:T(8,128)(2,1)} fusion(bf16[1024,512]{1,0:T(8,128)(2,1)} %all-gather.2.cloned.1.call-done, bf16[2048,256]{1,0:T(8,128)(2,1)} %param.13, bf16[2048,256]{1,0:T(8,128)(2,1)} %param.12), kind=kOutput, calls=%fused_computation | convolution fusion | flops 2153775104 | bytes 7340032 | tf_op jit(solution)/shard_map/dot_general | solution.py:21
  47.0 0.0 copy-start.3
  47.0 0.0 copy-start.5
  47.0 0.0 copy-start.4
  47.0 0.0 copy-start.1
  47.0 0.0 copy-start.2
  47.0 0.0 reduce-scatter.2.cloned.1.call-update
  47.0 0.0 all-reduce.3.cloned.1.call-start
  47.1 0.8 copy-done.3
  47.9 0.0 copy-done.5
  47.9 0.2 fusion.4
  48.1 0.0 copy-done.4
  48.1 0.2 fusion.3
  48.2 42.9 %reduce-scatter.2.cloned.1.call-done = bf16[256,2048]{1,0:T(8,128)(2,1)} async-done(((bf16[1024,2048]{1,0:T(8,128)(2,1)}), bf16[256,2048]{1,0:T(8,128)(2,1)}) %reduce-scatter.2.cloned.1.call-update) | async-done | bytes 1048592 | tf_op jit(solution)/shard_map/reduce_scatter | solution.py:27
  91.2 1.9 %collective-permute-start = (bf16[256,2048]{1,0:T(8,128)(2,1)}, bf16[256,2048]{1,0:T(8,128)(2,1)S(1)}, u32[]{:S(2)}, u32[]{:S(2)}) collective-permute-start(bf16[256,2048]{1,0:T(8,128)(2,1)} %reduce-scatter.2.cloned.1.call-done), channel_id=1, source_target_pairs={{0,0},{1,4},{2,8},{3,12},{4,1},{5,5},{6,9},{7,13},{8,2},{9,6},{10,... | collective-permute-start | bytes 3145736 | tf_op jit(solution)/shard_map/ppermute | solution.py:31
  93.0 0.6 pad_maximum_fusion.1
  93.7 0.0 copy-done
  93.7 0.0 copy-done.1
  93.7 1.1 convolution_convert_fusion.1
  94.8 0.0 all-reduce.3.cloned.1.call-update
  95.5 32.3 %all-reduce.3.cloned.1.call-done = (bf16[256,2,64]{0,2,1:T(8,128)(2,1)}, bf16[256,2,64]{0,2,1:T(8,128)(2,1)}) async-done(((bf16[256,2,64]{0,2,1:T(8,128)(2,1)}, bf16[256,2,64]{0,2,1:T(8,128)(2,1)}), (bf16[256,2,64]{0,2,1:T(8,128)(2,1)}, bf16[256,2,64]{0,2,1:T(8,128)(2,1)})) %all-reduce.3.cloned.1.call-update) | async-done | bytes 131088 | tf_op jit(solution)/shard_map/psum | solution.py:56
  127.8 1.0 fusion.5
  128.8 0.1 reshape.37
  128.9 17.0 %all_gather.7 = bf16[4,2,1024]{2,1,0:T(2,128)(2,1)S(1)} all-gather(bf16[1,2,1024]{2,1,0:T(2,128)(2,1)S(1)} %reshape.37), channel_id=1, replica_groups=mesh['groups'=2,'dp'=4,'tensor'=4] {'dp'}, dimensions={0}, use_global_device_ids=true | all-gather | bytes 20480 | tf_op jit(solution)/shard_map/all_gather | solution.py:78
  145.9 0.0 copy-done.2
  145.9 0.2 convolution_bitcast_fusion
  146.1 7.5 %psum.23 = f32[128,4]{0,1:T(4,128)S(1)} all-reduce(f32[128,4]{0,1:T(4,128)S(1)} %convolution_bitcast_fusion), channel_id=1, replica_groups=mesh['groups'=2,'dp'=4,'tensor'=4] {'tensor'}, use_global_device_ids=true, to_apply=%region_3.0 | all-reduce | flops 512 | bytes 4096 | tf_op jit(solution)/shard_map/psum | solution.py:81
  153.6 0.6 broadcast_multiply_fusion
  154.2 0.0 collective-permute-done
  154.2 1.0 copy.23
  (1 shorter events, 0.0 us)
Async XLA Ops:
  7.2 86.5 %copy-start = (bf16[256,2048]{1,0:T(8,128)(2,1)S(1)}, bf16[256,2048]{1,0:T(8,128)(2,1)}, u32[]{:S(2)}) copy-start(bf16[256,2048]{1,0:T(8,128)(2,1)} %param.9) | copy-start | bytes 3145732
  7.2 33.6 %all-gather.2.cloned.1.call-start = ((), (), s32[]{:S(2)}) async-start(), calls=%async_computation.1 | async-start | bytes 1310720 | tf_op jit(solution)/shard_map/all_gather | solution.py:22
  9.0 82.2 %reduce-scatter.2.cloned.1.call-start = ((), (), s32[]{:S(2)}) async-start(), calls=%async_computation.2 | async-start | bytes 5242880 | tf_op jit(solution)/shard_map/reduce_scatter | solution.py:27
  47.0 0.9 copy-start.3
  47.0 0.9 copy-start.5
  47.0 1.1 copy-start.4
  47.0 46.7 %copy-start.1 = (bf16[2048,128]{1,0:T(8,128)(2,1)S(1)}, bf16[2048,128]{1,0:T(8,128)(2,1)}, u32[]{:S(2)}) copy-start(bf16[2048,128]{1,0:T(8,128)(2,1)} %param.14) | copy-start | bytes 1572868
  47.0 98.9 %copy-start.2 = (bf16[128,2,1024]{2,1,0:T(2,128)(2,1)S(1)}, bf16[128,2,1024]{2,1,0:T(2,128)(2,1)}, u32[]{:S(2)}) copy-start(bf16[128,2,1024]{2,1,0:T(2,128)(2,1)} %param.17) | copy-start | bytes 1572868
  47.0 80.8 %all-reduce.3.cloned.1.call-start = ((), (), s32[]{:S(2)}) async-start(), calls=%async_computation.3 | async-start | bytes 262144 | tf_op jit(solution)/shard_map/psum | solution.py:56
  91.2 63.0 %collective-permute-start = (bf16[256,2048]{1,0:T(8,128)(2,1)}, bf16[256,2048]{1,0:T(8,128)(2,1)S(1)}, u32[]{:S(2)}, u32[]{:S(2)}) collective-permute-start(bf16[256,2048]{1,0:T(8,128)(2,1)} %reduce-scatter.2.cloned.1.call-done), channel_id=1, source_target_pairs={{0,0},{1,4},{2,8},{3,12},{4,1},{5,5},{6,9},{7,13},{8,2},{9,6},{10,... | collective-permute-start | bytes 3145736 | tf_op jit(solution)/shard_map/ppermute | solution.py:31
Sparse Core Ops, SparseCore 0:
  10.2 30.6 all-gather.1
  47.2 43.9 reduce-scatter.1
  95.0 32.8 all-reduce.2

commit v2 on v1

--- a/solution.py
+++ b/solution.py
@@ -1,6 +1,8 @@
 import jax
 import jax.numpy as jnp
 from jax import lax
+from jax.experimental import pallas as pl
+from jax.experimental.pallas import tpu as pltpu
 from jax.sharding import PartitionSpec as P
 
 
@@ -31,7 +33,7 @@
     return lax.ppermute(mine, ("dp", "tensor"), turn)
 
 
-def body(
+def plain(
     normed, grad_key, grad_value, weight_key, weight_value, proj_in, proj_out, lengths, queries
 ):
     grads = jnp.concatenate([grad_key, grad_value], axis=1)
@@ -82,6 +84,356 @@
     return (grad_input, scores)
 
 
+MESH = pl.DeviceIdType.MESH
+F32 = jnp.float32
+BF16 = jnp.bfloat16
+
+
+def visit(n):
+    rows = []
+    for d in range(n):
+        near = sorted(range(n), key=lambda j: (abs(j - d), min(j, n - 1 - j)))
+        rows.append(near)
+    return rows
+
+
+def pick(table, d, k):
+    value = jnp.int32(table[0][k])
+    for place in range(1, len(table)):
+        value = jnp.where(d == place, table[place][k], value)
+    return value
+
+
+def nt_dot(a, b):
+    return lax.dot_general(a, b, (((1,), (1,)), ((), ())), preferred_element_type=F32)
+
+
+def fused_kernel(
+    n,
+    length_ref, normed_ref, gk_ref, gv_ref, wk_ref, wv_ref, pin_ref, pout_ref, q_ref,
+    out_ref, score_ref,
+    grads, weights, normed, pin, pout, queries,
+    acc, c_send, c_recv, x_send, x_recv, f_send, f_recv,
+    sk_acc, sk_send, sk_recv, seqs, parts,
+    load_sem, g_send_sem, g_recv_sem, c_sem, x_sem, f_send_sem, f_recv_sem,
+    o_send_sem, o_recv_sem, sk_sem, s_send_sem, s_recv_sem, p_send_sem, p_recv_sem,
+):
+    group, d, t = lax.axis_index("groups"), lax.axis_index("dp"), lax.axis_index("tensor")
+    core, x = lax.rem(t, 2), lax.div(t, 2)
+    rows = gk_ref.shape[0]
+    rank = pout_ref.shape[2]
+    own_rows = rank // n
+    half = wk_ref.shape[0] // 2
+    quarter = half // 2
+    table = visit(n)
+    order = [pick(table, d, k) for k in range(n)]
+    at_core = (group, d, t + 1 - 2 * core)
+    at_x = (group, d, lax.rem(t + 2, 4))
+
+    def remote(src, dst, send, recv, where):
+        return pltpu.make_async_remote_copy(
+            src_ref=src, dst_ref=dst, send_sem=send, recv_sem=recv,
+            device_id=where, device_id_type=MESH,
+        )
+
+    loads = [
+        pltpu.make_async_copy(src, dst, load_sem.at[i])
+        for i, (src, dst) in enumerate(
+            [
+                (gk_ref, grads.at[d, 0]), (gv_ref, grads.at[d, 1]),
+                (wk_ref, weights.at[0]), (wv_ref, weights.at[1]),
+                (normed_ref, normed), (pin_ref, pin), (pout_ref, pout), (q_ref, queries),
+            ]
+        )
+    ]
+    for load in loads:
+        load.start()
+
+    barrier = pltpu.get_barrier_semaphore()
+    for step in range(1, n):
+        pl.semaphore_signal(barrier, 1, device_id=(group, lax.rem(d + step, n), t), device_id_type=MESH)
+        pl.semaphore_signal(barrier, 1, device_id=(group, d, lax.rem(t + step, n)), device_id_type=MESH)
+    pl.semaphore_wait(barrier, 2 * (n - 1))
+
+    def up(j, h, src):
+        return remote(src, grads.at[j, h], g_send_sem.at[0, j, h], g_recv_sem.at[j, h], (group, lax.rem(d + 1, n), t))
+
+    def down(j, h, src):
+        return remote(src, grads.at[j, h], g_send_sem.at[1, j, h], g_recv_sem.at[j, h], (group, lax.rem(d + n - 1, n), t))
+
+    def pass_on(k, finish=False):
+        j = order[k]
+        for h, own in enumerate((gk_ref, gv_ref)):
+            src = own if k == 0 else grads.at[j, h]
+            if k > 0 and not finish:
+                up(j, h, src).wait_recv()
+            for copy, more in ((up, (j <= d) & (d < n - 1)), (down, (j >= d) & (d > 0))):
+                @pl.when(more)
+                def _(copy=copy, src=src, h=h):
+                    if finish:
+                        copy(j, h, src).wait_send()
+                    else:
+                        copy(j, h, src).start()
+
+    def core_copy(k):
+        return remote(c_send.at[k], c_recv.at[k], c_sem.at[0, k], c_sem.at[1, k], at_core)
+
+    def x_copy(k):
+        return remote(x_send.at[k], x_recv.at[k], x_sem.at[0, k], x_sem.at[1, k], at_x)
+
+    def multiply(k):
+        j = order[k]
+        for sub in range(2):
+            start = pl.multiple_of((1 - core) * half + sub * quarter, quarter)
+            c_send[k, sub] = (
+                nt_dot(grads[j, 0], weights[0, pl.ds(start, quarter), :])
+                + nt_dot(grads[j, 1], weights[1, pl.ds(start, quarter), :])
+            ).astype(BF16)
+        core_copy(k).start()
+        for sub in range(2):
+            start = pl.multiple_of(core * half + sub * quarter, quarter)
+            acc[k, sub] = (
+                nt_dot(grads[j, 0], weights[0, pl.ds(start, quarter), :])
+                + nt_dot(grads[j, 1], weights[1, pl.ds(start, quarter), :])
+            )
+
+    def add_core(k):
+        core_copy(k).wait_recv()
+        x_send[k] = (acc[k, 1 - x] + c_recv[k, 1 - x].astype(F32)).astype(BF16)
+        x_copy(k).start()
+        acc[k, x] = acc[k, x] + c_recv[k, x].astype(F32)
+
+    def f_copy(k, source=None):
+        if source is None:
+            return remote(f_send.at[k], f_recv.at[d], f_send_sem.at[k], f_recv_sem.at[d], (group, order[k], t))
+        return remote(f_send.at[k], f_recv.at[source], f_send_sem.at[k], f_recv_sem.at[source], (group, order[k], t))
+
+    def add_x(k):
+        x_copy(k).wait_recv()
+        total = (acc[k, x] + x_recv[k].astype(F32)).astype(BF16)
+        if k == 0:
+            f_recv[d] = total
+        else:
+            f_send[k] = total
+            f_copy(k).start()
+
+    columns = pl.ds(pl.multiple_of(core * half + x * quarter, quarter), quarter)
+
+    def deliver(k, finish=False):
+        source = order[k]
+        if k > 0 and not finish:
+            f_copy(k, source).wait_recv()
+
+        @pl.when(source == t)
+        def _():
+            if not finish:
+                pltpu.make_async_copy(f_recv.at[source], out_ref.at[:, columns], o_recv_sem.at[t]).start()
+
+        @pl.when(source != t)
+        def _():
+            copy = remote(
+                f_recv.at[source], out_ref.at[:, columns], o_send_sem.at[k], o_recv_sem.at[t], (group, d, source)
+            )
+            if finish:
+                copy.wait_send()
+            else:
+                copy.start()
+
+    def sk_copy(i, where):
+        return remote(sk_send.at[i], sk_recv.at[i], sk_sem.at[0, i], sk_sem.at[1, i], where)
+
+    def sketch_parts():
+        for load in loads[4:7]:
+            load.wait()
+        sk_acc[:, : 2 * rank] = jnp.dot(normed[...], pin[...], preferred_element_type=F32)
+        sk_acc[:, 2 * rank :] = jnp.concatenate(
+            [
+                jnp.dot(grads[d, 0], pout[0], preferred_element_type=F32),
+                jnp.dot(grads[d, 1], pout[1], preferred_element_type=F32),
+            ],
+            axis=1,
+        )
+        sk_send[0] = sk_acc[...].astype(BF16)
+        sk_copy(0, at_core).start()
+
+    def sketch_x():
+        sk_copy(0, at_core).wait_recv()
+        sk_acc[...] = sk_acc[...] + sk_recv[0].astype(F32)
+        sk_send[1] = sk_acc[...].astype(BF16)
+        sk_copy(1, at_x).start()
+
+    def seq_copy(step, source=None):
+        slot = d if source is None else source
+        return remote(
+            seqs.at[slot], seqs.at[slot], s_send_sem.at[step], s_recv_sem.at[slot],
+            (group, lax.rem(d + step, n), t),
+        )
+
+    def sketch_seq():
+        sk_copy(1, at_x).wait_recv()
+        whole = (sk_acc[...] + sk_recv[1].astype(F32)).astype(BF16)
+        length = length_ref[0]
+        live = lax.broadcasted_iota(jnp.int32, (rows, 2 * rank), 0) < length
+        outs = jnp.where(live, whole[:, 2 * rank :].astype(F32), 0.0).astype(BF16)
+        c = lax.broadcasted_iota(jnp.int32, (2 * rank, 2 * own_rows), 0)
+        r = lax.broadcasted_iota(jnp.int32, (2 * rank, 2 * own_rows), 1)
+        chosen = (r // own_rows) * rank + t * own_rows + lax.rem(r, own_rows)
+        mine = jnp.dot(outs, (c == chosen).astype(F32).astype(BF16), preferred_element_type=F32).astype(BF16)
+        sums = lax.dot_general(
+            mine, whole[:, : 2 * rank], (((0,), (0,)), ((), ())), preferred_element_type=F32
+        )
+        scale = 1.0 / jnp.sqrt(jnp.full(sums.shape, length, jnp.int32).astype(F32))
+        seqs[d] = (sums * scale).astype(BF16)
+        for step in range(1, n):
+            seq_copy(step).start()
+
+    def part_copy(step, source=None):
+        slot = t if source is None else source
+        return remote(
+            parts.at[slot], parts.at[slot], p_send_sem.at[step], p_recv_sem.at[slot],
+            (group, d, lax.rem(t + step, n)),
+        )
+
+    def part_scores():
+        for step in range(1, n):
+            seq_copy(step, lax.rem(d + step, n)).wait_recv()
+        loads[7].wait()
+        wide = 2 * own_rows * rank
+        block = 2 * own_rows
+        f = lax.broadcasted_iota(jnp.int32, (2 * rank, wide), 1)
+        c = lax.broadcasted_iota(jnp.int32, (2 * rank, wide), 0)
+        spread = (c == (f // (own_rows * rank)) * rank + lax.rem(f, rank)).astype(F32).astype(BF16)
+        everything = jnp.concatenate([seqs[i] for i in range(n)], axis=0)
+        tall = jnp.dot(everything, spread, preferred_element_type=F32)
+        f = lax.broadcasted_iota(jnp.int32, (n * block, wide), 1)
+        r = lax.broadcasted_iota(jnp.int32, (n * block, wide), 0)
+        kept = jnp.where(lax.rem(r, block) == f // rank, tall, 0.0).astype(BF16)
+        s = lax.broadcasted_iota(jnp.int32, (8, n * block), 0)
+        r = lax.broadcasted_iota(jnp.int32, (8, n * block), 1)
+        flat = jnp.dot((r // block == s).astype(F32).astype(BF16), kept, preferred_element_type=F32).astype(BF16)
+        parts[t] = nt_dot(flat, queries[...])
+        for step in range(1, n):
+            part_copy(step).start()
+
+    def whole_scores():
+        for step in range(1, n):
+            part_copy(step, lax.rem(t + step, n)).wait_recv()
+        total = parts[0]
+        for i in range(1, n):
+            total = total + parts[i]
+        score_ref[...] = total * (1.0 / rank)
+
+    pass_on(0)
+    for load in loads[:4]:
+        load.wait()
+    multiply(0)
+    sketch_parts()
+    add_core(0)
+    sketch_x()
+    pass_on(1)
+    multiply(1)
+    add_x(0)
+    deliver(0)
+    pass_on(2)
+    add_core(1)
+    multiply(2)
+    sketch_seq()
+    add_x(1)
+    add_core(2)
+    pass_on(3)
+    multiply(3)
+    add_x(2)
+    add_core(3)
+    part_scores()
+    deliver(1)
+    add_x(3)
+    deliver(2)
+    deliver(3)
+    whole_scores()
+    for source in range(n):
+        remote(f_recv.at[0], out_ref.at[:, pl.ds(((source % 2) * 2 + source // 2) * quarter, quarter)],
+               o_send_sem.at[0], o_recv_sem.at[source], at_core).wait_recv()
+    for k in range(n):
+        pass_on(k, finish=True)
+        core_copy(k).wait_send()
+        x_copy(k).wait_send()
+        if k > 0:
+            f_copy(k).wait_send()
+            seq_copy(k).wait_send()
+            part_copy(k).wait_send()
+        deliver(k, finish=True)
+    sk_copy(0, at_core).wait_send()
+    sk_copy(1, at_x).wait_send()
+
+
+def body(
+    normed, grad_key, grad_value, weight_key, weight_value, proj_in, proj_out, lengths, queries
+):
+    n = lax.axis_size("dp")
+    rows, wide = normed.shape
+    depth = grad_key.shape[1]
+    rank = proj_out.shape[2]
+    count = queries.shape[0]
+    features = weight_key.shape[0]
+    if not (n == lax.axis_size("tensor") == 4 and lengths.shape[0] == 1 and features == wide):
+        return plain(
+            normed, grad_key, grad_value, weight_key, weight_value, proj_in, proj_out, lengths, queries
+        )
+    quarter = features // 4
+    flat_queries = queries.reshape(count, -1)
+    anywhere = pl.BlockSpec(memory_space=pl.ANY)
+    dma = pltpu.SemaphoreType.DMA
+    grad_input, scores = pl.pallas_call(
+        lambda *refs: fused_kernel(n, *refs),
+        out_shape=(
+            jax.ShapeDtypeStruct((rows, wide), BF16),
+            jax.ShapeDtypeStruct((8, count), F32),
+        ),
+        in_specs=[pl.BlockSpec(memory_space=pltpu.SMEM)] + [anywhere] * 8,
+        out_specs=(anywhere, pl.BlockSpec(memory_space=pltpu.VMEM)),
+        scratch_shapes=[
+            pltpu.VMEM((n, 2, rows, depth), BF16),
+            pltpu.VMEM((2, features, depth), BF16),
+            pltpu.VMEM(normed.shape, BF16),
+            pltpu.VMEM(proj_in.shape, BF16),
+            pltpu.VMEM(proj_out.shape, BF16),
+            pltpu.VMEM(flat_queries.shape, BF16),
+            pltpu.VMEM((n, 2, rows, quarter), F32),
+            pltpu.VMEM((n, 2, rows, quarter), BF16),
+            pltpu.VMEM((n, 2, rows, quarter), BF16),
+            pltpu.VMEM((n, rows, quarter), BF16),
+            pltpu.VMEM((n, rows, quarter), BF16),
+            pltpu.VMEM((n, rows, quarter), BF16),
+            pltpu.VMEM((n, rows, quarter), BF16),
+            pltpu.VMEM((rows, 4 * rank), F32),
+            pltpu.VMEM((2, rows, 4 * rank), BF16),
+            pltpu.VMEM((2, rows, 4 * rank), BF16),
+            pltpu.VMEM((n, 2 * rank // n, 2 * rank), BF16),
+            pltpu.VMEM((n, 8, count), F32),
+            dma((8,)),
+            dma((2, n, 2)),
+            dma((n, 2)),
+            dma((2, n)),
+            dma((2, n)),
+            dma((n,)),
+            dma((n,)),
+            dma((n,)),
+            dma((n,)),
+            dma((2, 2)),
+            dma((n,)),
+            dma((n,)),
+            dma((n,)),
+            dma((n,)),
+        ],
+        compiler_params=pltpu.CompilerParams(
+            collective_id=0, has_side_effects=True, vmem_limit_bytes=48 * 1024 * 1024
+        ),
+    )(
+        lengths, normed, grad_key, grad_value, weight_key, weight_value, proj_in, proj_out, flat_queries
+    )
+    return (grad_input, scores[:n].T)
+
+
 def solution(mesh):
     in_specs = (
         P(("groups", "dp"), "tensor"),

time: 162 us -> 82.7 us (0.51)
  the two profiles are of different devices: /device:TPU:0 before, /device:TPU:24 now
where the time goes in v2:
time: 82.7 us; the launch traced here: 82.4 us
  Pallas kernels  72.9 us (88%)
  local copies, waits for them, and re-layouts  8.1 us (10%)
  between operations  1.43 us (2%)
    pallas_call x1, Pallas kernels, body(): pl.pallas_call(lambda *refs: fused_kernel(n, *refs), out_shape=(jax.Shape...  72.9 us
    unnamed x15, local copies, waits for them, and re-layouts  7.52 us

profile of v2, /device:TPU:24, one launch (start us, length us, event | category | flops | bytes accessed | tf_op | source)
XLA Modules:
  0.0 82.4 jit_solution(604790247263658384)
XLA Ops:
  0.6 0.0 copy-start
  1.4 1.0 %copy.11.refs_7_ = bf16[2,256,64]{2,1,0:T(8,128)(2,1)S(1)} copy(bf16[2,256,64]{1,2,0:T(8,128)(2,1)} %param.15) | data formatting | bytes 131072 | tf_op args[6]
  2.3 0.0 copy-start.4
  2.4 1.2 %copy.12 = bf16[16,8,2,1024]{3,1,2,0:T(8,128)(2,1)S(1)} copy(bf16[16,8,2,1024]{3,2,1,0:T(2,128)(2,1)} %bitcast.5) | data formatting | bytes 1048576
  3.5 0.0 copy-done
  3.6 0.0 copy-done.4
  3.6 0.0 copy-start.1
  3.6 1.2 %copy-done.1 = bf16[2048,256]{1,0:T(8,128)(2,1)S(1)} copy-done((bf16[2048,256]{1,0:T(8,128)(2,1)S(1)}, bf16[2048,256]{1,0:T(8,128)(2,1)}, u32[]{:S(2)}) %copy-start.1) | copy-done | bytes 1048600
  4.8 0.0 copy-start.2
  4.8 1.2 %copy-done.2 = bf16[2048,256]{1,0:T(8,128)(2,1)S(1)} copy-done((bf16[2048,256]{1,0:T(8,128)(2,1)S(1)}, bf16[2048,256]{1,0:T(8,128)(2,1)}, u32[]{:S(2)}) %copy-start.2) | copy-done | bytes 1048600
  6.0 0.0 copy-start.3
  6.0 1.0 %copy-done.3 = bf16[2048,128]{1,0:T(8,128)(2,1)S(1)} copy-done((bf16[2048,128]{1,0:T(8,128)(2,1)S(1)}, bf16[2048,128]{1,0:T(8,128)(2,1)}, u32[]{:S(2)}) %copy-start.3) | copy-done | bytes 524312
  7.1 0.0 copy-start.5
  7.1 0.9 %copy-done.5 = bf16[256,256]{1,0:T(8,128)(2,1)S(1)} copy-done((bf16[256,256]{1,0:T(8,128)(2,1)S(1)}, bf16[256,256]{1,0:T(8,128)(2,1)}, u32[]{:S(2)}) %copy-start.5) | copy-done | bytes 131096
  8.0 72.9 %shard_map.104 = (bf16[256,2048]{1,0:T(8,128)(2,1)S(1)}, f32[8,128]{1,0:T(8,128)S(1)}) custom-call(s32[1]{0:T(128)S(6)} %copy.14.refs_0_, bf16[256,2048]{1,0:T(8,128)(2,1)S(1)} %copy-done, bf16[256,256]{1,0:T(8,128)(2,1)S(1)} %copy-done.4, bf16[256,256]{1,0:T(8,128)(2,1)S(1)} %copy-done.5, bf16[2048,256]{1,0:T(8,128)(2,1)S(1)} %copy-done.1, ...), custom_call_target="tpu_custom_call" | custom-call | tf_op jit(solution)/shard_map/pallas_call | solution.py:386
  80.9 0.6 slice_bitcast_fusion
  81.4 1.0 %copy.15 = bf16[256,2048]{1,0:T(8,128)(2,1)} copy(bf16[256,2048]{1,0:T(8,128)(2,1)S(1)} %get-tuple-element.8) | data formatting | bytes 2097152
Async XLA Ops:
  0.6 2.9 %copy-start = (bf16[256,2048]{1,0:T(8,128)(2,1)S(1)}, bf16[256,2048]{1,0:T(8,128)(2,1)}, u32[]{:S(2)}) copy-start(bf16[256,2048]{1,0:T(8,128)(2,1)} %refs_1_.1) | copy-start | bytes 3145732
  2.3 1.2 %copy-start.4 = (bf16[256,256]{1,0:T(8,128)(2,1)S(1)}, bf16[256,256]{1,0:T(8,128)(2,1)}, u32[]{:S(2)}) copy-start(bf16[256,256]{1,0:T(8,128)(2,1)} %refs_2_.1) | copy-start | bytes 393220
  3.6 1.2 %copy-start.1 = (bf16[2048,256]{1,0:T(8,128)(2,1)S(1)}, bf16[2048,256]{1,0:T(8,128)(2,1)}, u32[]{:S(2)}) copy-start(bf16[2048,256]{1,0:T(8,128)(2,1)} %refs_4_.1) | copy-start | bytes 3145732
  4.8 1.2 %copy-start.2 = (bf16[2048,256]{1,0:T(8,128)(2,1)S(1)}, bf16[2048,256]{1,0:T(8,128)(2,1)}, u32[]{:S(2)}) copy-start(bf16[2048,256]{1,0:T(8,128)(2,1)} %refs_5_.1) | copy-start | bytes 3145732
  6.0 1.0 %copy-start.3 = (bf16[2048,128]{1,0:T(8,128)(2,1)S(1)}, bf16[2048,128]{1,0:T(8,128)(2,1)}, u32[]{:S(2)}) copy-start(bf16[2048,128]{1,0:T(8,128)(2,1)} %refs_6_.1) | copy-start | bytes 1572868
  7.1 0.9 %copy-start.5 = (bf16[256,256]{1,0:T(8,128)(2,1)S(1)}, bf16[256,256]{1,0:T(8,128)(2,1)}, u32[]{:S(2)}) copy-start(bf16[256,256]{1,0:T(8,128)(2,1)} %refs_3_.1) | copy-start | bytes 393220

commit v3 on v2

--- a/solution.py
+++ b/solution.py
@@ -89,19 +89,36 @@
 BF16 = jnp.bfloat16
 
 
+CUTS = 2
+
+
 def visit(n):
     rows = []
     for d in range(n):
-        near = sorted(range(n), key=lambda j: (abs(j - d), min(j, n - 1 - j)))
-        rows.append(near)
+        far = [(j, h) for h in range(CUTS) for j in range(n) if j != d]
+        far.sort(key=lambda item: ((abs(item[0] - d) - 1) * CUTS + item[1], min(item[0], n - 1 - item[0])))
+        rows.append([(d, 0)] + far + [(d, h) for h in range(1, CUTS)])
     return rows
 
 
+def arrivals(n):
+    table = visit(n)
+    rows = []
+    for i in range(n):
+        far = [(s, h) for s in range(n) if s != i for h in range(CUTS)]
+        far.sort(key=lambda item: (table[item[0]].index((i, item[1])), abs(item[0] - i)))
+        rows.append(far)
+    return rows
+
+
 def pick(table, d, k):
-    value = jnp.int32(table[0][k])
-    for place in range(1, len(table)):
-        value = jnp.where(d == place, table[place][k], value)
-    return value
+    values = []
+    for part in range(2):
+        value = jnp.int32(table[0][k][part])
+        for place in range(1, len(table)):
+            value = jnp.where(d == place, table[place][k][part], value)
+        values.append(value)
+    return values
 
 
 def nt_dot(a, b):
@@ -121,12 +138,16 @@
     group, d, t = lax.axis_index("groups"), lax.axis_index("dp"), lax.axis_index("tensor")
     core, x = lax.rem(t, 2), lax.div(t, 2)
     rows = gk_ref.shape[0]
-    rank = pout_ref.shape[2]
+    rank = pout_ref.shape[1]
     own_rows = rank // n
     half = wk_ref.shape[0] // 2
     quarter = half // 2
     table = visit(n)
-    order = [pick(table, d, k) for k in range(n)]
+    items = n * CUTS
+    order = [pick(table, d, k) for k in range(items)]
+    coming = arrivals(n)
+    expected = [pick(coming, d, k) for k in range(items - CUTS)]
+    cut = rows // CUTS
     at_core = (group, d, t + 1 - 2 * core)
     at_x = (group, d, lax.rem(t + 2, 4))
 
@@ -139,8 +160,8 @@
     loads = [
         pltpu.make_async_copy(src, dst, load_sem.at[i])
         for i, (src, dst) in enumerate(
-            [
-                (gk_ref, grads.at[d, 0]), (gv_ref, grads.at[d, 1]),
+            [(src.at[pl.ds(h * cut, cut)], grads.at[d, h, v]) for v, src in enumerate((gk_ref, gv_ref)) for h in range(CUTS)]
+            + [
                 (wk_ref, weights.at[0]), (wv_ref, weights.at[1]),
                 (normed_ref, normed), (pin_ref, pin), (pout_ref, pout), (q_ref, queries),
             ]
@@ -155,25 +176,30 @@
         pl.semaphore_signal(barrier, 1, device_id=(group, d, lax.rem(t + step, n)), device_id_type=MESH)
     pl.semaphore_wait(barrier, 2 * (n - 1))
 
-    def up(j, h, src):
-        return remote(src, grads.at[j, h], g_send_sem.at[0, j, h], g_recv_sem.at[j, h], (group, lax.rem(d + 1, n), t))
-
-    def down(j, h, src):
-        return remote(src, grads.at[j, h], g_send_sem.at[1, j, h], g_recv_sem.at[j, h], (group, lax.rem(d + n - 1, n), t))
+    def up(j, h, v, src):
+        return remote(
+            src, grads.at[j, h, v], g_send_sem.at[0, j, h, v], g_recv_sem.at[j, h, v], (group, lax.rem(d + 1, n), t)
+        )
+
+    def down(j, h, v, src):
+        return remote(
+            src, grads.at[j, h, v], g_send_sem.at[1, j, h, v], g_recv_sem.at[j, h, v], (group, lax.rem(d + n - 1, n), t)
+        )
 
     def pass_on(k, finish=False):
-        j = order[k]
-        for h, own in enumerate((gk_ref, gv_ref)):
-            src = own if k == 0 else grads.at[j, h]
-            if k > 0 and not finish:
-                up(j, h, src).wait_recv()
+        own = k == 0 or k > items - CUTS
+        j, h = order[k]
+        for v, ref in enumerate((gk_ref, gv_ref)):
+            src = ref.at[pl.ds((0 if k == 0 else k - items + CUTS) * cut, cut)] if own else grads.at[j, h, v]
+            if not own and not finish:
+                up(j, h, v, src).wait_recv()
             for copy, more in ((up, (j <= d) & (d < n - 1)), (down, (j >= d) & (d > 0))):
                 @pl.when(more)
-                def _(copy=copy, src=src, h=h):
+                def _(copy=copy, src=src, v=v):
                     if finish:
-                        copy(j, h, src).wait_send()
+                        copy(j, h, v, src).wait_send()
                     else:
-                        copy(j, h, src).start()
+                        copy(j, h, v, src).start()
 
     def core_copy(k):
         return remote(c_send.at[k], c_recv.at[k], c_sem.at[0, k], c_sem.at[1, k], at_core)
@@ -182,19 +208,19 @@
         return remote(x_send.at[k], x_recv.at[k], x_sem.at[0, k], x_sem.at[1, k], at_x)
 
     def multiply(k):
-        j = order[k]
+        j, h = order[k]
         for sub in range(2):
             start = pl.multiple_of((1 - core) * half + sub * quarter, quarter)
             c_send[k, sub] = (
-                nt_dot(grads[j, 0], weights[0, pl.ds(start, quarter), :])
-                + nt_dot(grads[j, 1], weights[1, pl.ds(start, quarter), :])
+                nt_dot(grads[j, h, 0], weights[0, pl.ds(start, quarter), :])
+                + nt_dot(grads[j, h, 1], weights[1, pl.ds(start, quarter), :])
             ).astype(BF16)
         core_copy(k).start()
         for sub in range(2):
             start = pl.multiple_of(core * half + sub * quarter, quarter)
             acc[k, sub] = (
-                nt_dot(grads[j, 0], weights[0, pl.ds(start, quarter), :])
-                + nt_dot(grads[j, 1], weights[1, pl.ds(start, quarter), :])
+                nt_dot(grads[j, h, 0], weights[0, pl.ds(start, quarter), :])
+                + nt_dot(grads[j, h, 1], weights[1, pl.ds(start, quarter), :])
             )
 
     def add_core(k):
@@ -203,36 +229,37 @@
         x_copy(k).start()
         acc[k, x] = acc[k, x] + c_recv[k, x].astype(F32)
 
-    def f_copy(k, source=None):
-        if source is None:
-            return remote(f_send.at[k], f_recv.at[d], f_send_sem.at[k], f_recv_sem.at[d], (group, order[k], t))
-        return remote(f_send.at[k], f_recv.at[source], f_send_sem.at[k], f_recv_sem.at[source], (group, order[k], t))
+    def f_copy(k):
+        i, h = order[k]
+        return remote(f_send.at[k], f_recv.at[d, h], f_send_sem.at[k], f_recv_sem.at[d, h], (group, i, t))
 
     def add_x(k):
         x_copy(k).wait_recv()
         total = (acc[k, x] + x_recv[k].astype(F32)).astype(BF16)
-        if k == 0:
-            f_recv[d] = total
+        if k == 0 or k > items - CUTS:
+            f_recv[d, 0 if k == 0 else k - items + CUTS] = total
         else:
             f_send[k] = total
             f_copy(k).start()
 
     columns = pl.ds(pl.multiple_of(core * half + x * quarter, quarter), quarter)
 
-    def deliver(k, finish=False):
-        source = order[k]
-        if k > 0 and not finish:
-            f_copy(k, source).wait_recv()
+    def deliver(source, h, own=False, finish=False):
+        if not own and not finish:
+            remote(
+                f_send.at[0], f_recv.at[source, h], f_send_sem.at[0], f_recv_sem.at[source, h], (group, source, t)
+            ).wait_recv()
+        there = out_ref.at[pl.ds(pl.multiple_of(h * cut, cut), cut), columns]
 
         @pl.when(source == t)
         def _():
             if not finish:
-                pltpu.make_async_copy(f_recv.at[source], out_ref.at[:, columns], o_recv_sem.at[t]).start()
+                pltpu.make_async_copy(f_recv.at[source, h], there, o_recv_sem.at[t, h]).start()
 
         @pl.when(source != t)
         def _():
             copy = remote(
-                f_recv.at[source], out_ref.at[:, columns], o_send_sem.at[k], o_recv_sem.at[t], (group, d, source)
+                f_recv.at[source, h], there, o_send_sem.at[source, h], o_recv_sem.at[t, h], (group, d, source)
             )
             if finish:
                 copy.wait_send()
@@ -243,16 +270,13 @@
         return remote(sk_send.at[i], sk_recv.at[i], sk_sem.at[0, i], sk_sem.at[1, i], where)
 
     def sketch_parts():
-        for load in loads[4:7]:
+        for load in loads[6:9]:
             load.wait()
         sk_acc[:, : 2 * rank] = jnp.dot(normed[...], pin[...], preferred_element_type=F32)
-        sk_acc[:, 2 * rank :] = jnp.concatenate(
-            [
-                jnp.dot(grads[d, 0], pout[0], preferred_element_type=F32),
-                jnp.dot(grads[d, 1], pout[1], preferred_element_type=F32),
-            ],
-            axis=1,
-        )
+        for h in range(CUTS):
+            sk_acc[pl.ds(h * cut, cut), 2 * rank :] = jnp.concatenate(
+                [nt_dot(grads[d, h, 0], pout[0]), nt_dot(grads[d, h, 1], pout[1])], axis=1
+            )
         sk_send[0] = sk_acc[...].astype(BF16)
         sk_copy(0, at_core).start()
 
@@ -297,7 +321,7 @@
     def part_scores():
         for step in range(1, n):
             seq_copy(step, lax.rem(d + step, n)).wait_recv()
-        loads[7].wait()
+        loads[9].wait()
         wide = 2 * own_rows * rank
         block = 2 * own_rows
         f = lax.broadcasted_iota(jnp.int32, (2 * rank, wide), 1)
@@ -324,44 +348,70 @@
         score_ref[...] = total * (1.0 / rank)
 
     pass_on(0)
-    for load in loads[:4]:
+    for h in range(1, CUTS):
+        pass_on(items - CUTS + h)
+    for load in loads[:6]:
         load.wait()
     multiply(0)
+    pass_on(1)
+    add_core(0)
+    multiply(1)
+    pass_on(2)
     sketch_parts()
-    add_core(0)
-    sketch_x()
-    pass_on(1)
-    multiply(1)
-    add_x(0)
-    deliver(0)
-    pass_on(2)
     add_core(1)
     multiply(2)
+    pass_on(3)
+    sketch_x()
+    add_core(2)
+    multiply(3)
+    add_x(0)
+    pass_on(4)
+    add_core(3)
+    add_x(1)
+    multiply(4)
+    pass_on(5)
+    add_core(4)
+    multiply(5)
     sketch_seq()
-    add_x(1)
-    add_core(2)
-    pass_on(3)
-    multiply(3)
     add_x(2)
-    add_core(3)
+    pass_on(6)
+    add_core(5)
+    multiply(6)
+    add_x(3)
+    add_core(6)
+    multiply(7)
+    add_core(7)
+    deliver(d, 0, own=True)
     part_scores()
-    deliver(1)
-    add_x(3)
-    deliver(2)
-    deliver(3)
+    add_x(4)
+    deliver(*expected[0])
+    deliver(*expected[1])
+    add_x(5)
+    add_x(6)
+    deliver(*expected[2])
+    deliver(*expected[3])
+    add_x(7)
+    deliver(d, 1, own=True)
+    deliver(*expected[4])
+    deliver(*expected[5])
     whole_scores()
     for source in range(n):
-        remote(f_recv.at[0], out_ref.at[:, pl.ds(((source % 2) * 2 + source // 2) * quarter, quarter)],
-               o_send_sem.at[0], o_recv_sem.at[source], at_core).wait_recv()
-    for k in range(n):
+        for h in range(CUTS):
+            place = pl.ds(((source % 2) * 2 + source // 2) * quarter, quarter)
+            remote(f_recv.at[0, h], out_ref.at[pl.ds(h * cut, cut), place],
+                   o_send_sem.at[0, 0], o_recv_sem.at[source, h], at_core).wait_recv()
+    for k in range(items):
         pass_on(k, finish=True)
         core_copy(k).wait_send()
         x_copy(k).wait_send()
-        if k > 0:
+        if 0 < k <= items - CUTS:
             f_copy(k).wait_send()
-            seq_copy(k).wait_send()
-            part_copy(k).wait_send()
-        deliver(k, finish=True)
+    for k in range(1, n):
+        seq_copy(k).wait_send()
+        part_copy(k).wait_send()
+    for source in range(n):
+        for h in range(CUTS):
+            deliver(source, h, finish=True)
     sk_copy(0, at_core).wait_send()
     sk_copy(1, at_x).wait_send()
 
@@ -380,6 +430,7 @@
             normed, grad_key, grad_value, weight_key, weight_value, proj_in, proj_out, lengths, queries
         )
     quarter = features // 4
+    items, cut = n * CUTS, rows // CUTS
     flat_queries = queries.reshape(count, -1)
     anywhere = pl.BlockSpec(memory_space=pl.ANY)
     dma = pltpu.SemaphoreType.DMA
@@ -392,33 +443,33 @@
         in_specs=[pl.BlockSpec(memory_space=pltpu.SMEM)] + [anywhere] * 8,
         out_specs=(anywhere, pl.BlockSpec(memory_space=pltpu.VMEM)),
         scratch_shapes=[
-            pltpu.VMEM((n, 2, rows, depth), BF16),
+            pltpu.VMEM((n, CUTS, 2, cut, depth), BF16),
             pltpu.VMEM((2, features, depth), BF16),
             pltpu.VMEM(normed.shape, BF16),
             pltpu.VMEM(proj_in.shape, BF16),
-            pltpu.VMEM(proj_out.shape, BF16),
+            pltpu.VMEM((2, rank, depth), BF16),
             pltpu.VMEM(flat_queries.shape, BF16),
-            pltpu.VMEM((n, 2, rows, quarter), F32),
-            pltpu.VMEM((n, 2, rows, quarter), BF16),
-            pltpu.VMEM((n, 2, rows, quarter), BF16),
-            pltpu.VMEM((n, rows, quarter), BF16),
-            pltpu.VMEM((n, rows, quarter), BF16),
-            pltpu.VMEM((n, rows, quarter), BF16),
-            pltpu.VMEM((n, rows, quarter), BF16),
+            pltpu.VMEM((items, 2, cut, quarter), F32),
+            pltpu.VMEM((items, 2, cut, quarter), BF16),
+            pltpu.VMEM((items, 2, cut, quarter), BF16),
+            pltpu.VMEM((items, cut, quarter), BF16),
+            pltpu.VMEM((items, cut, quarter), BF16),
+            pltpu.VMEM((items, cut, quarter), BF16),
+            pltpu.VMEM((n, CUTS, cut, quarter), BF16),
             pltpu.VMEM((rows, 4 * rank), F32),
             pltpu.VMEM((2, rows, 4 * rank), BF16),
             pltpu.VMEM((2, rows, 4 * rank), BF16),
             pltpu.VMEM((n, 2 * rank // n, 2 * rank), BF16),
             pltpu.VMEM((n, 8, count), F32),
-            dma((8,)),
-            dma((2, n, 2)),
-            dma((n, 2)),
-            dma((2, n)),
-            dma((2, n)),
-            dma((n,)),
-            dma((n,)),
-            dma((n,)),
-            dma((n,)),
+            dma((10,)),
+            dma((2, n, CUTS, 2)),
+            dma((n, CUTS, 2)),
+            dma((2, items)),
+            dma((2, items)),
+            dma((items,)),
+            dma((n, CUTS)),
+            dma((n, CUTS)),
+            dma((n, CUTS)),
             dma((2, 2)),
             dma((n,)),
             dma((n,)),
@@ -426,10 +477,11 @@
             dma((n,)),
         ],
         compiler_params=pltpu.CompilerParams(
-            collective_id=0, has_side_effects=True, vmem_limit_bytes=48 * 1024 * 1024
+            collective_id=0, has_side_effects=True, vmem_limit_bytes=62 * 1024 * 1024
         ),
     )(
-        lengths, normed, grad_key, grad_value, weight_key, weight_value, proj_in, proj_out, flat_queries
+        lengths, normed, grad_key, grad_value, weight_key, weight_value, proj_in,
+        jnp.swapaxes(proj_out, 1, 2), flat_queries,
     )
     return (grad_input, scores[:n].T)
 

time: 82.7 us -> 68.5 us (0.83)
  the two profiles are of different devices: /device:TPU:24 before, /device:TPU:0 now
where the time goes in v3:
time: 68.5 us; the launch traced here: 68.3 us
  Pallas kernels  61.5 us (90%)
  local copies, waits for them, and re-layouts  5.52 us (8%)
  between operations  1.29 us (2%)
    pallas_call x1, Pallas kernels, body(): pl.pallas_call(lambda *refs: fused_kernel(n, *refs), out_shape=(jax.Shape...  61.5 us
    unnamed x2, local copies, waits for them, and re-layouts  4.26 us

profile of v3, /device:TPU:0, one launch (start us, length us, event | category | flops | bytes accessed | tf_op | source)
XLA Modules:
  0.0 68.3 jit_solution(4120588535585014475)
XLA Ops:
  1.3 2.0 %copy.11 = bf16[16,8,2,1024]{3,1,2,0:T(8,128)(2,1)} copy(bf16[16,8,2,1024]{3,2,1,0:T(2,128)(2,1)} %bitcast.6) | data formatting | bytes 1048576
  3.2 61.5 %shard_map.104 = (bf16[256,2048]{1,0:T(8,128)(2,1)}, f32[8,128]{1,0:T(8,128)}) custom-call(s32[1]{0:T(128)S(6)} %copy.13.refs_0_, bf16[256,2048]{1,0:T(8,128)(2,1)} %refs_1_.1, bf16[256,256]{1,0:T(8,128)(2,1)} %refs_2_.1, bf16[256,256]{1,0:T(8,128)(2,1)} %refs_3_.1, bf16[2048,256]{1,0:T(8,128)(2,1)} %refs_4_.1, bf16[2048,256]{1,0:T(8,128)(2,1)} %refs_5_.1, ...), custom_call_target="tpu_custom_call" | custom-call | tf_op jit(solution)/shard_map/pallas_call | solution.py:437
  64.7 1.3 %slice_bitcast_fusion = f32[128,4]{0,1:T(4,128)} fusion(f32[8,128]{1,0:T(8,128)} %get-tuple-element.5), kind=kLoop, calls=%fused_computation | loop fusion | bytes 4096 | tf_op jit(solution)/shard_map/transpose | solution.py:486
  66.0 2.3 %copy.14 = bf16[256,2048]{1,0:T(8,128)(2,1)} copy(bf16[256,2048]{1,0:T(8,128)(2,1)} %get-tuple-element.8) | data formatting | bytes 2097152

commit v4 on v3

--- a/solution.py
+++ b/solution.py
@@ -284,7 +284,15 @@
         sk_copy(0, at_core).wait_recv()
         sk_acc[...] = sk_acc[...] + sk_recv[0].astype(F32)
         sk_send[1] = sk_acc[...].astype(BF16)
-        sk_copy(1, at_x).start()
+        sk_half(1, sk_send, core, at_x).start()
+
+    def sk_half(i, src, part, where):
+        span = pl.ds(pl.multiple_of(part * (rows // 2), rows // 2), rows // 2)
+        return remote(src.at[1, span], sk_recv.at[1, span], sk_sem.at[0, i], sk_sem.at[1, i], where)
+
+    def sketch_turn():
+        sk_half(1, sk_send, core, at_x).wait_recv()
+        sk_half(2, sk_recv, core, at_core).start()
 
     def seq_copy(step, source=None):
         slot = d if source is None else source
@@ -294,7 +302,7 @@
         )
 
     def sketch_seq():
-        sk_copy(1, at_x).wait_recv()
+        sk_half(2, sk_recv, 1 - core, at_core).wait_recv()
         whole = (sk_acc[...] + sk_recv[1].astype(F32)).astype(BF16)
         length = length_ref[0]
         live = lax.broadcasted_iota(jnp.int32, (rows, 2 * rank), 0) < length
@@ -335,7 +343,7 @@
         s = lax.broadcasted_iota(jnp.int32, (8, n * block), 0)
         r = lax.broadcasted_iota(jnp.int32, (8, n * block), 1)
         flat = jnp.dot((r // block == s).astype(F32).astype(BF16), kept, preferred_element_type=F32).astype(BF16)
-        parts[t] = nt_dot(flat, queries[...])
+        parts[t] = nt_dot(flat[:, : wide // 2], queries[:, 0, :]) + nt_dot(flat[:, wide // 2 :], queries[:, 1, :])
         for step in range(1, n):
             part_copy(step).start()
 
@@ -345,7 +353,7 @@
         total = parts[0]
         for i in range(1, n):
             total = total + parts[i]
-        score_ref[...] = total * (1.0 / rank)
+        score_ref[...] = (total * (1.0 / rank))[:n]
 
     pass_on(0)
     for h in range(1, CUTS):
@@ -355,6 +363,7 @@
     multiply(0)
     pass_on(1)
     add_core(0)
+    multiply(items - 1)
     multiply(1)
     pass_on(2)
     sketch_parts()
@@ -365,33 +374,33 @@
     add_core(2)
     multiply(3)
     add_x(0)
+    add_x(1)
     pass_on(4)
     add_core(3)
-    add_x(1)
     multiply(4)
+    sketch_turn()
+    add_x(2)
     pass_on(5)
     add_core(4)
     multiply(5)
     sketch_seq()
-    add_x(2)
+    add_x(3)
     pass_on(6)
     add_core(5)
     multiply(6)
-    add_x(3)
+    add_x(4)
     add_core(6)
-    multiply(7)
     add_core(7)
     deliver(d, 0, own=True)
+    deliver(*expected[0])
+    add_x(5)
+    deliver(*expected[1])
+    add_x(6)
+    add_x(7)
+    deliver(d, 1, own=True)
     part_scores()
-    add_x(4)
-    deliver(*expected[0])
-    deliver(*expected[1])
-    add_x(5)
-    add_x(6)
     deliver(*expected[2])
     deliver(*expected[3])
-    add_x(7)
-    deliver(d, 1, own=True)
     deliver(*expected[4])
     deliver(*expected[5])
     whole_scores()
@@ -413,7 +422,8 @@
         for h in range(CUTS):
             deliver(source, h, finish=True)
     sk_copy(0, at_core).wait_send()
-    sk_copy(1, at_x).wait_send()
+    sk_half(1, sk_send, core, at_x).wait_send()
+    sk_half(2, sk_recv, core, at_core).wait_send()
 
 
 def body(
@@ -431,14 +441,14 @@
         )
     quarter = features // 4
     items, cut = n * CUTS, rows // CUTS
-    flat_queries = queries.reshape(count, -1)
+    flat_queries = queries
     anywhere = pl.BlockSpec(memory_space=pl.ANY)
     dma = pltpu.SemaphoreType.DMA
     grad_input, scores = pl.pallas_call(
         lambda *refs: fused_kernel(n, *refs),
         out_shape=(
             jax.ShapeDtypeStruct((rows, wide), BF16),
-            jax.ShapeDtypeStruct((8, count), F32),
+            jax.ShapeDtypeStruct((n, count), F32),
         ),
         in_specs=[pl.BlockSpec(memory_space=pltpu.SMEM)] + [anywhere] * 8,
         out_specs=(anywhere, pl.BlockSpec(memory_space=pltpu.VMEM)),
@@ -470,7 +480,7 @@
             dma((n, CUTS)),
             dma((n, CUTS)),
             dma((n, CUTS)),
-            dma((2, 2)),
+            dma((2, 3)),
             dma((n,)),
             dma((n,)),
             dma((n,)),
@@ -483,7 +493,7 @@
         lengths, normed, grad_key, grad_value, weight_key, weight_value, proj_in,
         jnp.swapaxes(proj_out, 1, 2), flat_queries,
     )
-    return (grad_input, scores[:n].T)
+    return (grad_input, scores.T)
 
 
 def solution(mesh):

time: 68.5 us -> 63.8 us (0.931)
  local copies, waits for them, and re-layouts: 5.52 us -> 2.89 us
  Pallas kernels: 61.5 us -> 59.5 us
    pallas_call x1, Pallas kernels: 61.5 us -> 59.5 us  [body(): pl.pallas_call(lambda *refs: fused_kernel(n, *refs), out_shape=(jax.Shape...]
    unnamed x2 -> x4, local copies, waits for them, and re-layouts: 4.26 us -> 2.89 us
    transpose x1 -> x0, local copies, waits for them, and re-layouts: 1.26 us -> none  [body(): return (grad_input, scores[:n].T)]
where the time goes in v4:
time: 63.8 us; the launch traced here: 63.7 us
  Pallas kernels  59.5 us (93%)
  local copies, waits for them, and re-layouts  2.89 us (5%)
  between operations  1.3 us (2%)
    pallas_call x1, Pallas kernels, body(): pl.pallas_call(lambda *refs: fused_kernel(n, *refs), out_shape=(jax.Shape...  59.5 us
    unnamed x4, local copies, waits for them, and re-layouts  2.89 us

profile of v4, /device:TPU:0, one launch (start us, length us, event | category | flops | bytes accessed | tf_op | source)
XLA Modules:
  0.0 63.7 jit_solution(10553316738184740840)
XLA Ops:
  1.3 59.5 %shard_map.104 = (bf16[256,2048]{1,0:T(8,128)(2,1)}, f32[4,128]{1,0:T(4,128)}) custom-call(s32[1]{0:T(128)S(6)} %copy.13.refs_0_, bf16[256,2048]{1,0:T(8,128)(2,1)} %refs_1_.1, bf16[256,256]{1,0:T(8,128)(2,1)} %refs_2_.1, bf16[256,256]{1,0:T(8,128)(2,1)} %refs_3_.1, bf16[2048,256]{1,0:T(8,128)(2,1)} %refs_4_.1, bf16[2048,256]{1,0:T(8,128)(2,1)} %refs_5_.1, ...), custom_call_target="tpu_custom_call" | custom-call | tf_op jit(solution)/shard_map/pallas_call | solution.py:447
  60.8 0.0 copy-start
  60.8 2.3 %copy.14 = bf16[256,2048]{1,0:T(8,128)(2,1)} copy(bf16[256,2048]{1,0:T(8,128)(2,1)} %get-tuple-element.8) | data formatting | bytes 2097152
  63.1 0.0 copy-done
  63.1 0.6 copy.15
Async XLA Ops:
  60.8 2.3 %copy-start = (f32[4,128]{1,0:T(4,128)S(1)}, f32[4,128]{1,0:T(4,128)}, u32[]{:S(2)}) copy-start(f32[4,128]{1,0:T(4,128)} %get-tuple-element.5) | copy-start | bytes 6148

commit v5 on v4

--- a/solution.py
+++ b/solution.py
@@ -391,18 +391,18 @@
     add_x(4)
     add_core(6)
     add_core(7)
+    add_x(5)
+    add_x(6)
+    deliver(*expected[0])
+    deliver(*expected[1])
     deliver(d, 0, own=True)
-    deliver(*expected[0])
-    add_x(5)
-    deliver(*expected[1])
-    add_x(6)
     add_x(7)
-    deliver(d, 1, own=True)
-    part_scores()
     deliver(*expected[2])
     deliver(*expected[3])
+    part_scores()
     deliver(*expected[4])
     deliver(*expected[5])
+    deliver(d, 1, own=True)
     whole_scores()
     for source in range(n):
         for h in range(CUTS):

time: 63.8 us -> 62.4 us (0.978)
  Pallas kernels: 59.5 us -> 58 us
    pallas_call x1, Pallas kernels: 59.5 us -> 58 us  [body(): pl.pallas_call(lambda *refs: fused_kernel(n, *refs), out_shape=(jax.Shape...]
where the time goes in v5:
time: 62.4 us; the launch traced here: 62.2 us
  Pallas kernels  58 us (93%)
  local copies, waits for them, and re-layouts  2.89 us (5%)
  between operations  1.3 us (2%)
    pallas_call x1, Pallas kernels, body(): pl.pallas_call(lambda *refs: fused_kernel(n, *refs), out_shape=(jax.Shape...  58 us
    unnamed x4, local copies, waits for them, and re-layouts  2.89 us

profile of v5, /device:TPU:0, one launch (start us, length us, event | category | flops | bytes accessed | tf_op | source)
XLA Modules:
  0.0 62.2 jit_solution(7675925916893872716)
XLA Ops:
  1.3 58.0 %shard_map.104 = (bf16[256,2048]{1,0:T(8,128)(2,1)}, f32[4,128]{1,0:T(4,128)}) custom-call(s32[1]{0:T(128)S(6)} %copy.13.refs_0_, bf16[256,2048]{1,0:T(8,128)(2,1)} %refs_1_.1, bf16[256,256]{1,0:T(8,128)(2,1)} %refs_2_.1, bf16[256,256]{1,0:T(8,128)(2,1)} %refs_3_.1, bf16[2048,256]{1,0:T(8,128)(2,1)} %refs_4_.1, bf16[2048,256]{1,0:T(8,128)(2,1)} %refs_5_.1, ...), custom_call_target="tpu_custom_call" | custom-call | tf_op jit(solution)/shard_map/pallas_call | solution.py:447
  59.3 0.0 copy-start
  59.3 2.3 %copy.14 = bf16[256,2048]{1,0:T(8,128)(2,1)} copy(bf16[256,2048]{1,0:T(8,128)(2,1)} %get-tuple-element.8) | data formatting | bytes 2097152
  61.6 0.0 copy-done
  61.6 0.6 copy.15
Async XLA Ops:
  59.3 2.3 %copy-start = (f32[4,128]{1,0:T(4,128)S(1)}, f32[4,128]{1,0:T(4,128)}, u32[]{:S(2)}) copy-start(f32[4,128]{1,0:T(4,128)} %get-tuple-element.5) | copy-start | bytes 6148
